TPU v7x, 256 devices: a whole 4x4x8 slice. The times are simulated.
256 devices in a mesh: dp: 16 (over y, x), ctx: 16 (over z, core).
Axes of the slice: x: 4, y: 4, z: 8, core: 2. Of those that a mesh axis runs over, the one named last changes fastest.
Arguments:
- hidden_in: bfloat16 [16, 3072, 16384], P('dp', 'ctx'), may hold values from -8 to 8
- queries: bfloat16 [16, 3072, 1024], P('dp', 'ctx'), may hold values from -14 to 14
- grad_out: bfloat16 [16, 3072, 1024], P('dp', 'ctx'), may hold values from -6 to 6
- w_key: bfloat16 [16384, 128], P('dp'), may hold values from -1 to 1
- w_value: bfloat16 [16384, 128], P('dp'), may hold values from -0.046875 to 0.046875
- stretch_order: int32 [32], replicated, may hold values from 0 to 31, each once
- doc_lengths: int32 [16, 8], P('dp'), may hold values from 1 to 1536, 3072 in all within a row
Outputs:
- query_grad: bfloat16 [16, 3072, 1024], P('dp', 'ctx')
- key_weight_grad: float32 [16384, 128], P('dp')
- value_weight_grad: float32 [16384, 128], P('dp')
Inputs may be any that keep to these rules, and one draw needn't show every extreme that they name: `stretch_order`: every block number appears exactly once. `doc_lengths`: each sequence's lengths sum to 3072, and one of them is 1536.
All inputs are finite; a program needn't handle non-finite values.
Results may differ from a plain program's by a relative error of at most 0.03.
Values may be sent and summed in bfloat16 or wider, within the bound.
A program may use at most 128 MiB of HBM per device.

v0:
```python
import math
import jax
import jax.numpy as jnp
from jax import lax
from jax.sharding import PartitionSpec as P


def table_lookup(slots, table):
    choices_all = jnp.arange(table.shape[0], dtype=jnp.int32)
    return jnp.sum(jnp.where(slots[:, None] == choices_all[None, :], table[None, :], 0), axis=1)


def place_and_doc(stored, stretch_order, stretch_rows, doc_ends):
    place = (
        table_lookup(stored // stretch_rows, stretch_order) * stretch_rows + stored % stretch_rows
    )
    documents = jnp.sum((place[:, None] >= doc_ends[None, :]).astype(jnp.int32), axis=1)
    return (place, documents)


def attention_grads(query_rows, key_rows, value_rows, cotangent, allowed, head_count, head_dim):
    row_count = query_rows.shape[0]
    score_scale = 1.0 / math.sqrt(head_dim)
    query_heads = jnp.transpose(query_rows.reshape(row_count, head_count, head_dim), (1, 0, 2))
    cot_heads = jnp.transpose(cotangent.reshape(row_count, head_count, head_dim), (1, 0, 2))

    def one_head(running, items):
        query_one, cot_one = items
        scores = (
            jnp.dot(query_one, jnp.transpose(key_rows), preferred_element_type=jnp.float32)
            * score_scale
        )
        masked = jnp.where(allowed, scores, -jnp.inf)
        row_max = jnp.max(masked, axis=-1, keepdims=True)
        expsum = jnp.where(allowed, jnp.exp(masked - row_max), 0.0)
        probabilities = expsum / jnp.sum(expsum, axis=-1, keepdims=True)
        probs_low = probabilities.astype(jnp.bfloat16)
        attended = jnp.dot(probs_low, value_rows, preferred_element_type=jnp.float32)
        delta_rows = jnp.sum(cot_one.astype(jnp.float32) * attended, axis=-1)
        dprob = jnp.dot(cot_one, jnp.transpose(value_rows), preferred_element_type=jnp.float32)
        dscore = (probabilities * (dprob - delta_rows[:, None])).astype(jnp.bfloat16)
        query_grad = (
            jnp.dot(dscore, key_rows, preferred_element_type=jnp.float32) * score_scale
        ).astype(jnp.bfloat16)
        key_grad = (
            lax.dot_general(
                dscore, query_one, (((0,), (0,)), ((), ())), preferred_element_type=jnp.float32
            )
            * score_scale
        )
        value_grad = lax.dot_general(
            probs_low, cot_one, (((0,), (0,)), ((), ())), preferred_element_type=jnp.float32
        )
        return (running + jnp.concatenate([key_grad, value_grad], axis=1), query_grad)

    start_sum = jnp.zeros((key_rows.shape[0], 2 * head_dim), jnp.float32)
    kv_grads, query_grad = lax.scan(one_head, start_sum, (query_heads, cot_heads))
    return (
        jnp.transpose(query_grad, (1, 0, 2)).reshape(row_count, head_count * head_dim),
        kv_grads,
    )


def on_device(hidden_in, queries, grad_out, w_key, w_value, stretch_order, doc_lengths):
    inputs = hidden_in[0]
    row_count = inputs.shape[0]
    stretch_rows = row_count // 2
    head_dim = w_key.shape[1]
    head_count = queries.shape[2] // head_dim
    ctx_count = lax.axis_size("ctx")
    seq_rows = row_count * ctx_count
    stacked = jnp.concatenate([w_key, w_value], axis=1)
    columns = inputs
    projected = jnp.dot(
        columns,
        lax.all_gather(stacked, "dp", axis=0, tiled=True),
        preferred_element_type=jnp.float32,
    ).astype(jnp.bfloat16)
    gathered = lax.all_gather(projected, "ctx", axis=0, tiled=True)
    doc_ends = jnp.cumsum(doc_lengths[0])
    every_row = jnp.arange(seq_rows, dtype=jnp.int32)
    own_rows = lax.axis_index("ctx") * row_count + jnp.arange(row_count, dtype=jnp.int32)
    key_place, key_docs = place_and_doc(every_row, stretch_order, stretch_rows, doc_ends)
    query_place, query_docs = place_and_doc(own_rows, stretch_order, stretch_rows, doc_ends)
    allowed = (key_place[None, :] <= query_place[:, None]) & (
        key_docs[None, :] == query_docs[:, None]
    )
    query_grad, kv_partial = attention_grads(
        queries[0],
        gathered[:, :head_dim],
        gathered[:, head_dim:],
        grad_out[0],
        allowed,
        head_count,
        head_dim,
    )
    kv_grads = lax.psum_scatter(
        kv_partial.astype(jnp.bfloat16), "ctx", scatter_dimension=0, tiled=True
    )
    columns = inputs
    partial_rows = lax.psum_scatter(
        lax.dot_general(
            columns, kv_grads, (((0,), (0,)), ((), ())), preferred_element_type=jnp.float32
        ).astype(jnp.bfloat16),
        "dp",
        scatter_dimension=0,
        tiled=True,
    )
    weight_grads = lax.psum(partial_rows, "ctx").astype(jnp.float32)
    return (
        query_grad.reshape(1, row_count, head_count * head_dim),
        weight_grads[:, :head_dim],
        weight_grads[:, head_dim:],
    )


def solution(mesh):
    return jax.shard_map(
        on_device,
        mesh=mesh,
        in_specs=(
            P("dp", "ctx", None),
            P("dp", "ctx", None),
            P("dp", "ctx", None),
            P("dp", None),
            P("dp", None),
            P(),
            P("dp", None),
        ),
        out_specs=(P("dp", "ctx", None), P("dp", None), P("dp", None)),
        check_vma=False,
    )
```

profile of v0, /device:TPU:1, one launch (start us, length us, event | category | flops | bytes accessed | tf_op | source)
XLA Modules:
  0.0 494.5 jit_solution(5097747195582043551)
XLA Ops:
  7.2 1.9 pad_maximum_fusion
  9.2 81.4 %all-gather.3.cloned.1.call-done = bf16[16384,256]{1,0:T(8,128)(2,1)} async-done(((bf16[1024,256]{1,0:T(8,128)(2,1)}), bf16[16384,256]{1,0:T(8,128)(2,1)}) %all-gather.3.cloned.1.call-update) | async-done | bytes 8388624 | tf_op jit(solution)/shard_map/all_gather | solution.py:76
  90.6 7.6 %fusion.33 = bf16[192,256]{1,0:T(8,128)(2,1)} fusion(bf16[16384,256]{1,0:T(8,128)(2,1)} %all-gather.3.cloned.1.call-done, bf16[1,192,16384]{2,1,0:T(8,128)(2,1)} %param.9), kind=kOutput, calls=%fused_computation.39 | convolution fusion | flops 1610661888 | bytes 14778368 | tf_op jit(solution)/shard_map/dot_general | solution.py:74
  99.1 0.8 copy.23
  99.9 1.1 copy.31
  101.2 1.3 convert_reduce_fusion.1
  102.5 0.8 select_reduce_fusion
  103.3 1.3 convert_reduce_fusion
  104.6 33.1 %all-gather.5.cloned.1.call-done = bf16[3072,256]{1,0:T(8,128)(2,1)} async-done(((bf16[192,256]{1,0:T(8,128)(2,1)}), bf16[3072,256]{1,0:T(8,128)(2,1)}) %all-gather.5.cloned.1.call-update) | async-done | bytes 1572880 | tf_op jit(solution)/shard_map/all_gather | solution.py:79
  137.7 2.6 fusion.48
  140.3 75.2 %while.13 = (s32[]{:T(128)}, f32[3072,256]{0,1:T(8,128)S(1)}, bf16[8,192,128]{2,1,0:T(8,128)(2,1)}, bf16[8,192,128]{2,1,0:T(8,128)(2,1)}, bf16[3072,128]{1,0:T(8...) while((s32[]{:T(128)}, f32[3072,256]{0,1:T(8,128)S(1)}, ...), condition=%wide.region_9.10_spmd.clone, body=%wide.region_5.9_spmd.clone.sunk | while | flops 922410432 | bytes 42505748 | solution.py:57
  140.3 1.9 fusion.87
  143.0 0.8 fusion.89
  146.3 1.1 fusion.93
  147.4 1.2 convolution_multiply_fusion.5
  148.6 1.1 maximum_add_fusion.2
  149.7 1.9 fusion.87
  152.4 0.8 fusion.89
  155.7 1.1 fusion.93
  156.8 1.2 convolution_multiply_fusion.5
  158.0 1.1 maximum_add_fusion.2
  159.1 1.9 fusion.87
  161.0 0.8 fusion.88
  161.8 0.8 fusion.89
  165.1 1.1 fusion.93
  166.2 1.2 convolution_multiply_fusion.5
  167.4 1.1 maximum_add_fusion.2
  168.5 1.9 fusion.87
  170.4 0.8 fusion.88
  171.2 0.8 fusion.89
  174.5 1.1 fusion.93
  175.6 1.2 convolution_multiply_fusion.5
  176.8 1.1 maximum_add_fusion.2
  177.9 1.9 fusion.87
  180.6 0.8 fusion.89
  183.9 1.1 fusion.93
  185.0 1.2 convolution_multiply_fusion.5
  186.2 1.1 maximum_add_fusion.2
  187.3 1.9 fusion.87
  189.2 0.8 fusion.88
  190.0 0.8 fusion.89
  193.3 1.1 fusion.93
  194.4 1.2 convolution_multiply_fusion.5
  195.6 1.1 maximum_add_fusion.2
  196.7 1.9 fusion.87
  199.4 0.8 fusion.89
  202.7 1.1 fusion.93
  203.8 1.2 convolution_multiply_fusion.5
  205.0 1.1 maximum_add_fusion.2
  206.1 1.9 fusion.87
  208.8 0.8 fusion.89
  212.1 1.1 fusion.93
  213.2 1.2 convolution_multiply_fusion.5
  214.4 1.1 maximum_add_fusion.2
  215.5 1.4 convert_element_type.40
  216.8 2.6 copy.28
  219.5 53.6 %reduce-scatter.7.cloned.1.call-done = bf16[192,256]{1,0:T(8,128)(2,1)} async-done(((bf16[3072,256]{1,0:T(8,128)(2,1)}), bf16[192,256]{1,0:T(8,128)(2,1)}) %reduce-scatter.7.cloned.1.call-update) | async-done | bytes 98320
  273.1 8.4 %fusion.26 = bf16[16384,256]{0,1:T(8,128)(2,1)} fusion(bf16[192,256]{1,0:T(8,128)(2,1)} %reduce-scatter.7.cloned.1.call-done, bf16[1,192,16384]{2,1,0:T(8,128)(2,1)} %param.9), kind=kOutput, calls=%fused_computation.34 | convolution fusion | flops 1614807040 | bytes 14778368 | tf_op jit(solution)/shard_map/dot_general | solution.py:102
  281.7 90.6 %reduce-scatter.5.cloned.1.call-done = bf16[1024,256]{0,1:T(8,128)(2,1)} async-done(((bf16[16384,256]{0,1:T(8,128)(2,1)}), bf16[1024,256]{0,1:T(8,128)(2,1)}) %reduce-scatter.5.cloned.1.call-update) | async-done | bytes 524304 | tf_op jit(solution)/shard_map/reduce_scatter | solution.py:101
  372.6 0.9 reshape_reshape.3
  373.5 111.3 %all-reduce.2.cloned.1.call-done = bf16[1024,256]{0,1:T(8,128)(2,1)} async-done(((bf16[1024,256]{0,1:T(8,128)(2,1)}), bf16[1024,256]{0,1:T(8,128)(2,1)}) %all-reduce.2.cloned.1.call-update) | async-done | bytes 524304 | tf_op jit(solution)/shard_map/psum | solution.py:109
  484.9 1.1 fusion.49
  486.0 1.0 copy.27
  487.0 1.0 copy.26
  (122 shorter events, 25.0 us)
Async XLA Ops:
  7.2 83.4 %all-gather.3.cloned.1.call-start = ((), (), s32[]{:S(2)}) async-start(), calls=%async_computation.2 | async-start | bytes 8912896 | tf_op jit(solution)/shard_map/all_gather | solution.py:76
  9.1 89.2 %copy-start.7 = (s32[1,8]{1,0:T(1,128)S(1)}, s32[1,8]{1,0:T(1,128)}, u32[]{:S(2)}) copy-start(s32[1,8]{1,0:T(1,128)} %param.15) | copy-start | bytes 100
  9.1 89.9 %copy-start.3 = (bf16[1,192,1024]{2,1,0:T(8,128)(2,1)S(1)}, bf16[1,192,1024]{2,1,0:T(8,128)(2,1)}, u32[]{:S(2)}) copy-start(bf16[1,192,1024]{2,1,0:T(8,128)(2,1)} %param.10) | copy-start | bytes 1179652
  9.1 128.6 %all-gather.5.cloned.1.call-start = ((), (), s32[]{:S(2)}) async-start(), calls=%async_computation.3 | async-start | bytes 1671168 | tf_op jit(solution)/shard_map/all_gather | solution.py:79
  98.2 2.9 copy-start.6
  98.3 174.9 %reduce-scatter.7.cloned.1.call-start = ((), (), s32[]{:S(2)}) async-start(), calls=%async_computation.6 | async-start | bytes 1671168
  140.3 1.9 copy-start.2
  140.3 1.9 copy-start.5
  143.0 1.1 copy-start
  145.2 1.1 copy-start.1
  149.7 1.9 copy-start.2
  149.7 1.9 copy-start.5
  152.4 1.1 copy-start
  154.6 1.1 copy-start.1
  159.1 1.9 copy-start.2
  159.1 1.9 copy-start.5
  161.8 1.1 copy-start
  164.0 1.1 copy-start.1
  168.5 1.9 copy-start.2
  168.5 1.9 copy-start.5
  171.2 1.1 copy-start
  173.4 1.1 copy-start.1
  177.9 1.9 copy-start.2
  177.9 1.9 copy-start.5
  180.6 1.1 copy-start
  182.8 1.1 copy-start.1
  187.3 1.9 copy-start.2
  187.3 1.9 copy-start.5
  190.0 1.1 copy-start
  192.2 1.1 copy-start.1
  196.7 1.9 copy-start.2
  196.7 1.9 copy-start.5
  199.4 1.1 copy-start
  201.6 1.1 copy-start.1
  206.1 1.9 copy-start.2
  206.1 1.9 copy-start.5
  208.8 1.1 copy-start
  211.0 1.1 copy-start.1
  219.5 152.8 %reduce-scatter.5.cloned.1.call-start = ((), (), s32[]{:S(2)}) async-start(), calls=%async_computation.4 | async-start | bytes 8912896 | tf_op jit(solution)/shard_map/reduce_scatter | solution.py:101
  281.6 90.7 %copy-start.4 = (bf16[8,192,128]{2,1,0:T(8,128)(2,1)S(1)}, bf16[8,192,128]{2,1,0:T(8,128)(2,1)}, u32[]{:S(2)}) copy-start(bf16[8,192,128]{2,1,0:T(8,128)(2,1)} %get-tuple-element.46) | copy-start | bytes 1179652
  281.6 203.2 %all-reduce.2.cloned.1.call-start = ((), (), s32[]{:S(2)}) async-start(), calls=%async_computation.5 | async-start | bytes 1048576 | tf_op jit(solution)/shard_map/psum | solution.py:109
Sparse Core Ops, SparseCore 0:
  11.0 79.5 all-gather.2
  98.4 39.2 all-gather.4
  219.6 53.5 reduce-scatter.6
  281.7 90.5 reduce-scatter.4
  374.6 110.2 all-reduce.1
where the time goes:
time: 496 us; the launch traced here: 495 us
  waiting for transfers between devices  370 us (75%)
  matrix products  61.1 us (12%)
  other arithmetic  28.8 us (6%)
  local copies, waits for them, and re-layouts  19.4 us (4%)
  between operations  13.9 us (3%)
    psum x1, waiting for transfers between devices, on_device(): weight_grads = lax.psum(partial_rows, 'ctx').astype(jnp.float32)  111 us
    reduce_scatter x1, waiting for transfers between devices, on_device(): lax.psum_scatter(lax.dot_general(columns, kv_grads, (((0,), (0,)), ((), (...  90.6 us
    all_gather x1, waiting for transfers between devices, on_device(): lax.all_gather(stacked, 'dp', axis=0, tiled=True)  81.4 us
    unnamed x6, waiting for transfers between devices  53.7 us
    all_gather x1, waiting for transfers between devices, on_device(): gathered = lax.all_gather(projected, 'ctx', axis=0, tiled=True)  33.1 us
    dot_general x8, matrix products, one_head(): jnp.dot(query_one, jnp.transpose(key_rows), preferred_element_type=jnp.fl...  15 us
  transfers between devices with their start and end apart: 5, of which 5 were waited for; matrix products, arithmetic and copies ran while one was open for 1% of the time, Pallas kernels for 0%

commit v1 on v0

--- a/solution.py
+++ b/solution.py
@@ -73,7 +73,9 @@
     columns = inputs
     projected = jnp.dot(
         columns,
-        lax.all_gather(stacked, "dp", axis=0, tiled=True),
+        jnp.concatenate(
+            lax.all_to_all(jnp.stack([stacked] * lax.axis_size("dp")), "dp", 0, 0), axis=0
+        ),
         preferred_element_type=jnp.float32,
     ).astype(jnp.bfloat16)
     gathered = lax.all_gather(projected, "ctx", axis=0, tiled=True)

time: 496 us -> 582 us (1.17)
  blocking collectives: 0 us -> 102 us
  waiting for transfers between devices: 370 us -> 291 us
  other arithmetic: 28.8 us -> 65.4 us
  matrix products: 61.1 us -> 93.6 us
  local copies, waits for them, and re-layouts: 19.4 us -> 11.8 us
    all_to_all x0 -> x1, blocking collectives: none -> 102 us  [on_device(): lax.all_to_all(jnp.stack([stacked] * lax.axis_size('dp')), 'dp', 0, 0)]
    all_gather x1 -> x0, waiting for transfers between devices: 81.4 us -> none  [on_device(): lax.all_gather(stacked, 'dp', axis=0, tiled=True)]
    add x8, other arithmetic: 8.47 us -> 35.8 us  [one_head(): running + jnp.concatenate([key_grad, value_grad], axis=1)]
    dot_general x8, matrix products: 3.42 us -> 18.9 us  [one_head(): lax.dot_general(probs_low, cot_one, (((0,), (0,)), ((), ())), preferred_e...]
    dot_general x8, matrix products: 8.62 us -> 17.7 us  [one_head(): jnp.dot(dscore, key_rows, preferred_element_type=jnp.float32) * score_scale]
    while x64 -> x0, local copies, waits for them, and re-layouts: 7.9 us -> none
    dot_general x8, matrix products: 4.4 us -> 10.9 us  [one_head(): jnp.dot(probs_low, value_rows, preferred_element_type=jnp.float32)]
    dot_general x8, matrix products: 3.88 us -> 10.2 us  [one_head(): jnp.dot(cot_one, jnp.transpose(value_rows), preferred_element_type=jnp.fl...]
  transfers between devices with their start and end apart: 5 -> 4, of which waited for: 5 -> 4; matrix products, arithmetic and copies ran while one was open for 1% -> 1% of each run, Pallas kernels for 0% -> 0%
where the time goes in v1:
time: 582 us; the launch traced here: 579 us
  waiting for transfers between devices  291 us (50%)
  blocking collectives  102 us (18%)
  matrix products  93.6 us (16%)
  other arithmetic  65.4 us (11%)
  between operations  13.9 us (2%)
  local copies, waits for them, and re-layouts  11.8 us (2%)
    psum x1, waiting for transfers between devices, on_device(): weight_grads = lax.psum(partial_rows, 'ctx').astype(jnp.float32)  110 us
    all_to_all x1, blocking collectives, on_device(): lax.all_to_all(jnp.stack([stacked] * lax.axis_size('dp')), 'dp', 0, 0)  102 us
    reduce_scatter x1, waiting for transfers between devices, on_device(): lax.psum_scatter(lax.dot_general(columns, kv_grads, (((0,), (0,)), ((), (...  90.8 us
    unnamed x5, waiting for transfers between devices  53.7 us
    all_gather x1, waiting for transfers between devices, on_device(): gathered = lax.all_gather(projected, 'ctx', axis=0, tiled=True)  36.4 us
    add x8, other arithmetic, one_head(): running + jnp.concatenate([key_grad, value_grad], axis=1)  35.8 us
    dot_general x8, matrix products, one_head(): lax.dot_general(probs_low, cot_one, (((0,), (0,)), ((), ())), preferred_e...  18.9 us
    dot_general x8, matrix products, one_head(): jnp.dot(dscore, key_rows, preferred_element_type=jnp.float32) * score_scale  17.7 us
  transfers between devices with their start and end apart: 4, of which 4 were waited for; matrix products, arithmetic and copies ran while one was open for 1% of the time, Pallas kernels for 0%

profile of v1, /device:TPU:1, one launch (start us, length us, event | category | flops | bytes accessed | tf_op | source)
XLA Modules:
  0.0 578.7 jit_solution(14378515027988148759)
XLA Ops:
  9.1 102.4 %all_to_all.5 = bf16[16,1024,256]{2,1,0:T(8,128)(2,1)S(1)} all-to-all(bf16[16,1024,256]{2,1,0:T(8,128)(2,1)S(1)} %stack.2), channel_id=1, replica_groups=mesh['dp'=16,'ctx'=16] {'dp'}, dimensions={0} | all-to-all | bytes 16777216 | tf_op jit(solution)/shard_map/all_to_all | solution.py:77
  111.6 2.7 fusion.33
  118.0 36.4 %all-gather.2.cloned.1.call-done = bf16[3072,256]{1,0:T(8,128)(2,1)} async-done(((bf16[192,256]{1,0:T(8,128)(2,1)}), bf16[3072,256]{1,0:T(8,128)(2,1)}) %all-gather.2.cloned.1.call-update) | async-done | bytes 1572880 | tf_op jit(solution)/shard_map/all_gather | solution.py:81
  154.4 2.4 fusion.48
  156.8 143.1 %while.13 = (s32[]{:T(128)}, f32[3072,256]{0,1:T(8,128)}, bf16[8,192,128]{2,1,0:T(8,128)(2,1)}, bf16[8,192,128]{2,1,0:T(8,128)(2,1)}, bf16[3072,128]{1,0:T(8,128...) while((s32[]{:T(128)}, f32[3072,256]{0,1:T(8,128)}, ...), condition=%wide.region_9.10_spmd.clone, body=%wide.region_5.9_spmd.clone.sunk | while | flops 922410432 | bytes 36164232 | solution.py:57
  156.8 1.9 fusion.87
  158.6 1.5 fusion.88
  160.1 1.6 fusion.89
  161.7 1.4 fusion.91
  165.6 2.4 fusion.90
  168.0 3.6 maximum_add_fusion.2
  171.6 2.2 fusion.93
  173.8 1.9 fusion.87
  175.7 1.5 fusion.88
  177.2 1.6 fusion.89
  178.8 1.4 fusion.91
  182.6 2.4 fusion.90
  185.0 4.6 maximum_add_fusion.2
  189.6 2.2 fusion.93
  191.8 1.9 fusion.87
  193.7 1.5 fusion.88
  195.2 1.6 fusion.89
  196.8 1.4 fusion.91
  200.7 2.4 fusion.90
  203.0 4.6 maximum_add_fusion.2
  207.6 2.2 fusion.93
  209.8 1.9 fusion.87
  211.7 1.5 fusion.88
  213.2 1.6 fusion.89
  214.8 1.4 fusion.91
  218.7 2.4 fusion.90
  221.0 4.6 maximum_add_fusion.2
  225.6 2.2 fusion.93
  227.8 1.9 fusion.87
  229.7 1.5 fusion.88
  231.2 1.6 fusion.89
  232.8 1.4 fusion.91
  236.7 2.4 fusion.90
  239.0 4.6 maximum_add_fusion.2
  243.6 2.2 fusion.93
  245.8 1.9 fusion.87
  247.7 1.5 fusion.88
  249.2 1.6 fusion.89
  254.7 2.4 fusion.90
  257.0 4.6 maximum_add_fusion.2
  261.6 2.2 fusion.93
  263.8 1.9 fusion.87
  265.7 1.5 fusion.88
  267.2 1.6 fusion.89
  272.7 2.4 fusion.90
  275.0 4.6 maximum_add_fusion.2
  279.6 2.2 fusion.93
  281.8 1.9 fusion.87
  283.7 1.5 fusion.88
  285.2 1.6 fusion.89
  290.7 2.4 fusion.90
  293.0 4.6 maximum_add_fusion.2
  297.6 2.2 fusion.93
  299.8 2.1 convert_element_type.40
  302.0 1.6 copy.28
  303.6 53.6 %reduce-scatter.7.cloned.1.call-done = bf16[192,256]{1,0:T(8,128)(2,1)} async-done(((bf16[3072,256]{1,0:T(8,128)(2,1)}), bf16[192,256]{1,0:T(8,128)(2,1)}) %reduce-scatter.7.cloned.1.call-update) | async-done | bytes 98320
  357.2 8.4 %fusion.26 = bf16[16384,256]{0,1:T(8,128)(2,1)} fusion(bf16[192,256]{1,0:T(8,128)(2,1)} %reduce-scatter.7.cloned.1.call-done, bf16[1,192,16384]{2,1,0:T(8,128)(2,1)} %param.9), kind=kOutput, calls=%fused_computation.34 | convolution fusion | flops 1614807040 | bytes 14778368 | tf_op jit(solution)/shard_map/dot_general | solution.py:104
  365.8 90.8 %reduce-scatter.5.cloned.1.call-done = bf16[1024,256]{0,1:T(8,128)(2,1)} async-done(((bf16[16384,256]{0,1:T(8,128)(2,1)}), bf16[1024,256]{0,1:T(8,128)(2,1)}) %reduce-scatter.5.cloned.1.call-update) | async-done | bytes 524304 | tf_op jit(solution)/shard_map/reduce_scatter | solution.py:103
  458.8 110.2 %all-reduce.2.cloned.1.call-done = bf16[1024,256]{0,1:T(8,128)(2,1)} async-done(((bf16[1024,256]{0,1:T(8,128)(2,1)}), bf16[1024,256]{0,1:T(8,128)(2,1)}) %all-reduce.2.cloned.1.call-update) | async-done | bytes 524304 | tf_op jit(solution)/shard_map/psum | solution.py:111
  (62 shorter events, 35.1 us)
Async XLA Ops:
  7.2 147.2 %all-gather.2.cloned.1.call-start = ((), (), s32[]{:S(2)}) async-start(), calls=%async_computation.3 | async-start | bytes 1671168 | tf_op jit(solution)/shard_map/all_gather | solution.py:81
  8.3 103.3 %slice-start = ((s8[6291456]{0:T(1024)(128)(4,1)}), s8[2097152]{0:T(1024)(128)(4,1)S(1)}, s32[]{:S(2)}) async-start(s8[6291456]{0:T(1024)(128)(4,1)} %bitcast.78), calls=%async_computation.7 | async-start | bytes 4194304
  9.1 102.4 %slice-start.1 = ((s8[6291456]{0:T(1024)(128)(4,1)}), s8[4194304]{0:T(1024)(128)(4,1)S(1)}, s32[]{:S(2)}) async-start(s8[6291456]{0:T(1024)(128)(4,1)} %bitcast.78), calls=%async_computation.8 | async-start | bytes 8388608
  111.6 2.8 copy-start.3
  111.6 3.0 copy-start
  111.6 3.9 copy-start.1
  114.3 2.1 copy-start.2
  114.3 243.0 %reduce-scatter.7.cloned.1.call-start = ((), (), s32[]{:S(2)}) async-start(), calls=%async_computation.6 | async-start | bytes 1671168
  303.6 153.0 %reduce-scatter.5.cloned.1.call-start = ((), (), s32[]{:S(2)}) async-start(), calls=%async_computation.4 | async-start | bytes 8912896 | tf_op jit(solution)/shard_map/reduce_scatter | solution.py:103
  365.7 203.3 %all-reduce.2.cloned.1.call-start = ((), (), s32[]{:S(2)}) async-start(), calls=%async_computation.5 | async-start | bytes 1048576 | tf_op jit(solution)/shard_map/psum | solution.py:111
Sparse Core Ops, SparseCore 0:
  114.4 39.9 all-gather.1
  303.7 53.5 reduce-scatter.6
  365.8 90.6 reduce-scatter.4
  458.8 110.1 all-reduce.1
